TPU v7x, 32 devices: a whole 2x2x4 slice. The times are simulated.
32 devices in a mesh: parts: 2 (over y), leaf: 4 (over z), inner: 2 (over x), sub: 2 (over core).
Axes of the slice: x: 2, y: 2, z: 4, core: 2. Of those that a mesh axis runs over, the one named last changes fastest.
Arguments:
- points: bfloat16 [8192, 256], P(('parts', 'leaf', 'inner', 'sub')), parts along dimension 0, may hold values from -0.5 to 0.5
- exemplars: bfloat16 [8, 1024, 256], P(('parts', 'leaf')), parts along dimension 0, may hold values from -0.5 to 0.5
- selection: int32 [2, 8, 1024], P(None, ('parts', 'leaf')), parts along dimension 1, may hold values from 0 to 2047, as said below
Outputs:
- gains: float32 [2, 8, 2048], P(None, ('parts', 'leaf')), parts along dimension 1
- cover: float32 [8192], P(('parts', 'leaf', 'inner', 'sub')), parts along dimension 0
There are 2 independent parts, one for each index of `parts`. A program takes and returns all parts, laid end to end along the dimension named above; each array names one. Nothing has to cross between parts.
Inputs may be any that keep to these rules, and one draw needn't show every extreme that they name: `selection`: each row holds distinct values; the rows of level l are equal for all groups g with the same g // 2 ** (l + 1).
All inputs are finite; a program needn't handle non-finite values.
Results may differ from a plain program's by a relative error of at most 0.0003.
Values may be sent and summed in bfloat16 or wider, within the bound.
A program may use at most 64 MiB of HBM per device.

v0:
```python
import jax
import jax.numpy as jnp
from jax import lax
from jax.sharding import PartitionSpec as P


def swapped(x, axis, apart):
    return lax.ppermute(x, axis, [(i, i ^ 1 << apart) for i in range(lax.axis_size(axis))])


def on_device(points, exemplars, selection):
    current = exemplars[0]
    levels = selection.shape[0]
    leaf_index = lax.axis_index("leaf")
    own_sims = jnp.dot(points, current.T, preferred_element_type=jnp.float32)
    gain_terms = []
    for height in range(levels):
        partner = swapped(current, "leaf", height)
        partner_sims = jnp.dot(points, partner.T, preferred_element_type=jnp.float32)
        is_upper = leaf_index // 2**height % 2 == 1
        coverage = jnp.max(own_sims, 1)[:, None]
        own_gain = jnp.sum(jnp.maximum(own_sims - coverage, 0.0), 0)
        partner_gain = jnp.sum(jnp.maximum(partner_sims - coverage, 0.0), 0)
        first_gain = jnp.where(is_upper, partner_gain, own_gain)
        second_gain = jnp.where(is_upper, own_gain, partner_gain)
        gain_terms.append(jnp.concatenate([first_gain, second_gain], 0))
        picked = selection[height, 0]
        first_sims = jnp.where(is_upper, partner_sims, own_sims)
        second_sims = jnp.where(is_upper, own_sims, partner_sims)
        own_sims = jnp.take(jnp.concatenate([first_sims, second_sims], 1), picked, axis=1)
        if height + 1 < levels:
            first_rows = jnp.where(is_upper, partner, current)
            second_rows = jnp.where(is_upper, current, partner)
            current = jnp.take(jnp.concatenate([first_rows, second_rows], 0), picked, axis=0)
    cover = jnp.max(own_sims, 1)
    group_rows = []
    for height in range(levels):
        running = gain_terms[height]
        for shift_bit in range(height + 1):
            running = running + swapped(running, "leaf", shift_bit)
        group_rows.append(running)
    gains = lax.psum(jnp.stack(group_rows), ("inner", "sub"))
    return (gains[:, None, :], cover)


def solution(mesh):
    placed = (
        P(("parts", "leaf", "inner", "sub"), None),
        P(("parts", "leaf"), None, None),
        P(None, ("parts", "leaf"), None),
    )
    return jax.shard_map(
        on_device,
        mesh=mesh,
        in_specs=placed,
        out_specs=(P(None, ("parts", "leaf"), None), P(("parts", "leaf", "inner", "sub"))),
        check_vma=False,
    )
```

profile of v0, /device:TPU:0, one launch (start us, length us, event | category | flops | bytes accessed | tf_op | source)
XLA Modules:
  0.0 71.4 jit_solution(17099203640189343693)
XLA Ops:
  0.7 3.1 %collective-permute-start = (bf16[1024,256]{1,0:T(8,128)(2,1)}, bf16[1024,256]{1,0:T(8,128)(2,1)S(1)}, u32[]{:S(2)}, u32[]{:S(2)}) collective-permute-start(bf16[1024,256]{1,0:T(8,128)(2,1)} %bitcast.32), channel_id=1, source_target_pairs={{0,4},{4,0},{8,12},{12,8},{1,5},{5,1},{9,13},{13,9},{2,6},{6,2},{1... | collective-permute-start | bytes 1572872 | tf_op jit(solution)/shard_map/ppermute | solution.py:8
  3.7 0.7 fusion.8
  4.5 0.7 compare_select_fusion
  5.2 1.5 %fusion.9 = (f32[256]{0:T(256)S(1)}, f32[256,1024]{1,0:T(8,128)S(1)}) fusion(bf16[256,256]{1,0:T(8,128)(2,1)S(1)} %copy-done, bf16[1,1024,256]{2,1,0:T(8,128)(2,1)} %param.6), kind=kOutput, calls=%fused_computation.42 | convolution fusion | flops 134479616 | bytes 1704960 | tf_op jit(solution)/shard_map/dot_general | solution.py:15
  6.7 9.2 %collective-permute-done = bf16[1024,256]{1,0:T(8,128)(2,1)S(1)} collective-permute-done((bf16[1024,256]{1,0:T(8,128)(2,1)}, bf16[1024,256]{1,0:T(8,128)(2,1)S(1)}, u32[]{:S(2)}, u32[]{:S(2)}) %collective-permute-start) | collective-permute-done | bytes 524320 | tf_op jit(solution)/shard_map/ppermute | solution.py:8
  16.0 3.9 %gather_fusion = bf16[1024,256]{1,0:T(8,128)(2,1)S(1)} fusion(bf16[2048,256]{1,0:T(8,128)(2,1)S(1)} %pad_maximum_fusion.2, s32[1024]{0:T(1024)S(1)} %broadcast_clamp_fusion), kind=kCustom, calls=%fused_computation.2 | custom fusion | bytes 1052672 | tf_op jit(solution)/shard_map/jit(_take)/gather | solution.py:34
  20.0 1.0 %broadcast_select_fusion = bf16[1024,256]{1,0:T(8,128)(2,1)} fusion(bf16[1024,256]{1,0:T(8,128)(2,1)S(1)} %gather_fusion, pred[1024]{0:T(1024)(128)(4,1)S(1)} %compare_and_fusion.1), kind=kLoop, calls=%fused_computation.17 | loop fusion | flops 262144 | bytes 1049600 | tf_op jit(solution)/shard_map/jit(_take)/select_n | solution.py:34
  21.0 2.8 %collective-permute-start.2 = (bf16[1024,256]{1,0:T(8,128)(2,1)}, bf16[1024,256]{1,0:T(8,128)(2,1)}, u32[]{:S(2)}, u32[]{:S(2)}) collective-permute-start(bf16[1024,256]{1,0:T(8,128)(2,1)} %broadcast_select_fusion), channel_id=1, source_target_pairs={{0,8},{4,12},{8,0},{12,4},{1,9},{5,13},{9,1},{13,5},{2,10},{6,14},... | collective-permute-start | bytes 1572872 | tf_op jit(solution)/shard_map/ppermute | solution.py:8
  23.7 0.5 maximum_reduce_fusion.2
  24.2 1.5 %pad_maximum_fusion = f32[256,2048]{1,0:T(8,128)} fusion(f32[256,1024]{1,0:T(8,128)S(1)} %get-tuple-element.11, f32[256,1024]{1,0:T(8,128)S(1)} %get-tuple-element.12), kind=kLoop, calls=%fused_computation.3 | loop fusion | flops 524288 | bytes 4194304 | tf_op jit(solution)/shard_map/concatenate | solution.py:30
  25.7 1.9 %copy.10 = f32[256,2048]{0,1:T(8,128)S(1)} copy(f32[256,2048]{1,0:T(8,128)} %pad_maximum_fusion) | data formatting | bytes 4194304 | tf_op jit(solution)/shard_map/concatenate | solution.py:30
  27.6 3.5 %gather_fusion.1 = f32[1024,256]{1,0:T(8,128)S(1)} fusion(f32[256,2048]{0,1:T(8,128)S(1)} %copy.10, s32[1024]{0:T(1024)S(1)} %fusion.2), kind=kCustom, calls=%fused_computation.clone | custom fusion | bytes 2101248 | tf_op jit(solution)/shard_map/jit(_take)/gather | solution.py:30
  31.5 1.6 %collective-permute-start.1 = (f32[2048]{0:T(1024)S(1)}, f32[2048]{0:T(1024)S(1)}, u32[]{:S(2)}, u32[]{:S(2)}) collective-permute-start(f32[2048]{0:T(1024)S(1)} %pad_maximum_fusion.4), channel_id=1, source_target_pairs={{0,4},{4,0},{8,12},{12,8},{1,5},{5,1},{9,13},{13,9},{2,6},{6,2},{1... | collective-permute-start | bytes 24584 | tf_op jit(solution)/shard_map/ppermute | solution.py:8
  33.3 1.9 %collective-permute-done.1 = f32[2048]{0:T(1024)S(1)} collective-permute-done((f32[2048]{0:T(1024)S(1)}, f32[2048]{0:T(1024)S(1)}, u32[]{:S(2)}, u32[]{:S(2)}) %collective-permute-start.1) | collective-permute-done | bytes 8224 | tf_op jit(solution)/shard_map/ppermute | solution.py:8
  35.2 11.4 %collective-permute-done.2 = bf16[1024,256]{1,0:T(8,128)(2,1)} collective-permute-done((bf16[1024,256]{1,0:T(8,128)(2,1)}, bf16[1024,256]{1,0:T(8,128)(2,1)}, u32[]{:S(2)}, u32[]{:S(2)}) %collective-permute-start.2) | collective-permute-done | bytes 524320 | tf_op jit(solution)/shard_map/ppermute | solution.py:8
  46.6 1.5 %bitcast_select_fusion.1 = (f32[256,1024]{1,0:T(8,128)S(1)}, f32[256,1024]{1,0:T(8,128)S(1)}, f32[1024]{0:T(1024)S(1)}, f32[1024]{0:T(1024)S(1)}) fusion(f32[1024,256]{0,1:T(8,128)S(1)} %copy.11, pred[1024]{0:T(1024)(128)(4,1)S(1)} %compare_and_fusion.1, pred[]{:T(512)S(6)} %eq.10, f32[256]{0:T(256)S(1)} %bitcast_reduce_fusion.1, ...), kind=kOutput, calls=%fused_computation.9 | convolution fusion | flops 136574976 | bytes 3811329 | tf_op jit(solution)/shard_map/dot_general | solution.py:19
  48.1 0.6 collective-permute-start.3
  48.7 1.5 %pad_maximum_fusion.1 = f32[256,2048]{1,0:T(8,128)} fusion(f32[256,1024]{1,0:T(8,128)S(1)} %get-tuple-element.8, f32[256,1024]{1,0:T(8,128)S(1)} %get-tuple-element.7), kind=kLoop, calls=%fused_computation.4 | loop fusion | flops 524288 | bytes 4194304 | tf_op jit(solution)/shard_map/concatenate | solution.py:30
  50.2 1.9 %copy.12 = f32[256,2048]{0,1:T(8,128)S(1)} copy(f32[256,2048]{1,0:T(8,128)} %pad_maximum_fusion.1) | data formatting | bytes 4194304 | tf_op jit(solution)/shard_map/concatenate | solution.py:30
  52.1 3.5 %gather_fusion.2 = f32[1024,256]{1,0:T(8,128)S(1)} fusion(f32[256,2048]{0,1:T(8,128)S(1)} %copy.12, s32[1024]{0:T(1024)S(1)} %fusion.3), kind=kCustom, calls=%fused_computation.1.clone | custom fusion | bytes 2101248 | tf_op jit(solution)/shard_map/jit(_take)/gather | solution.py:30
  55.6 3.5 %collective-permute-start.4 = (f32[2048]{0:T(1024)S(1)}, f32[2048]{0:T(1024)S(1)}, u32[]{:S(2)}, u32[]{:S(2)}) collective-permute-start(f32[2048]{0:T(1024)S(1)} %fusion.6), channel_id=1, source_target_pairs={{0,8},{4,12},{8,0},{12,4},{1,9},{5,13},{9,1},{13,5},{2,10},{6,14},... | collective-permute-start | bytes 24584 | tf_op jit(solution)/shard_map/ppermute | solution.py:8
  59.1 0.8 %bitcast_reduce_fusion = f32[256]{0:T(256)} fusion(f32[1024,256]{1,0:T(8,128)S(1)} %gather_fusion.2, pred[1024]{0:T(1024)(128)(4,1)S(1)} %compare_and_fusion), kind=kLoop, calls=%fused_computation.7 | loop fusion | flops 524032 | bytes 1050624 | tf_op jit(solution)/shard_map/reduce_max | solution.py:35
  59.8 0.8 %collective-permute-done.4 = f32[2048]{0:T(1024)S(1)} collective-permute-done((f32[2048]{0:T(1024)S(1)}, f32[2048]{0:T(1024)S(1)}, u32[]{:S(2)}, u32[]{:S(2)}) %collective-permute-start.4) | collective-permute-done | bytes 8224 | tf_op jit(solution)/shard_map/ppermute | solution.py:8
  60.7 10.7 %psum.7 = f32[2,1,2048]{2,1,0:T(1,128)} all-reduce(f32[2,1,2048]{2,1,0:T(1,128)S(1)} %broadcast_in_dim.26), channel_id=1, replica_groups=mesh['parts'=2,'leaf'=4,'inner'=2,'sub'=2] {'inner','sub'}, use_global_device_ids=true, to_apply=%region_6.8 | all-reduce | flops 4096 | bytes 32768 | tf_op jit(solution)/shard_map/psum | solution.py:42
  (23 shorter events, 0.7 us)
Async XLA Ops:
  0.6 4.6 %copy-start = (bf16[256,256]{1,0:T(8,128)(2,1)S(1)}, bf16[256,256]{1,0:T(8,128)(2,1)}, u32[]{:S(2)}) copy-start(bf16[256,256]{1,0:T(8,128)(2,1)} %param.5) | copy-start | bytes 393220
  0.6 15.2 %copy-start.1 = (bf16[1,1024,256]{2,1,0:T(8,128)(2,1)S(1)}, bf16[1,1024,256]{2,1,0:T(8,128)(2,1)}, u32[]{:S(2)}) copy-start(bf16[1,1024,256]{2,1,0:T(8,128)(2,1)} %param.6) | copy-start | bytes 1572868
  0.7 15.2 %collective-permute-start = (bf16[1024,256]{1,0:T(8,128)(2,1)}, bf16[1024,256]{1,0:T(8,128)(2,1)S(1)}, u32[]{:S(2)}, u32[]{:S(2)}) collective-permute-start(bf16[1024,256]{1,0:T(8,128)(2,1)} %bitcast.32), channel_id=1, source_target_pairs={{0,4},{4,0},{8,12},{12,8},{1,5},{5,1},{9,13},{13,9},{2,6},{6,2},{1... | collective-permute-start | bytes 1572872 | tf_op jit(solution)/shard_map/ppermute | solution.py:8
  21.0 25.6 %collective-permute-start.2 = (bf16[1024,256]{1,0:T(8,128)(2,1)}, bf16[1024,256]{1,0:T(8,128)(2,1)}, u32[]{:S(2)}, u32[]{:S(2)}) collective-permute-start(bf16[1024,256]{1,0:T(8,128)(2,1)} %broadcast_select_fusion), channel_id=1, source_target_pairs={{0,8},{4,12},{8,0},{12,4},{1,9},{5,13},{9,1},{13,5},{2,10},{6,14},... | collective-permute-start | bytes 1572872 | tf_op jit(solution)/shard_map/ppermute | solution.py:8
  31.5 3.7 %collective-permute-start.1 = (f32[2048]{0:T(1024)S(1)}, f32[2048]{0:T(1024)S(1)}, u32[]{:S(2)}, u32[]{:S(2)}) collective-permute-start(f32[2048]{0:T(1024)S(1)} %pad_maximum_fusion.4), channel_id=1, source_target_pairs={{0,4},{4,0},{8,12},{12,8},{1,5},{5,1},{9,13},{13,9},{2,6},{6,2},{1... | collective-permute-start | bytes 24584 | tf_op jit(solution)/shard_map/ppermute | solution.py:8
  48.1 7.5 %collective-permute-start.3 = (f32[2048]{0:T(1024)S(1)}, f32[2048]{0:T(1024)S(1)}, u32[]{:S(2)}, u32[]{:S(2)}) collective-permute-start(f32[2048]{0:T(1024)S(1)} %pad_maximum_fusion.5), channel_id=1, source_target_pairs={{0,4},{4,0},{8,12},{12,8},{1,5},{5,1},{9,13},{13,9},{2,6},{6,2},{1... | collective-permute-start | bytes 24584 | tf_op jit(solution)/shard_map/ppermute | solution.py:8
  55.6 5.1 %collective-permute-start.4 = (f32[2048]{0:T(1024)S(1)}, f32[2048]{0:T(1024)S(1)}, u32[]{:S(2)}, u32[]{:S(2)}) collective-permute-start(f32[2048]{0:T(1024)S(1)} %fusion.6), channel_id=1, source_target_pairs={{0,8},{4,12},{8,0},{12,4},{1,9},{5,13},{9,1},{13,5},{2,10},{6,14},... | collective-permute-start | bytes 24584 | tf_op jit(solution)/shard_map/ppermute | solution.py:8
where the time goes:
time: 71.8 us; the launch traced here: 71.4 us
  waiting for transfers between devices  23.3 us (32%)
  local copies, waits for them, and re-layouts  15.8 us (22%)
  starting transfers between devices  11.5 us (16%)
  blocking collectives  10.7 us (15%)
  other arithmetic  5.85 us (8%)
  matrix products  3.42 us (5%)
  between operations  0.84 us (1%)
    ppermute x5, waiting for transfers between devices, swapped(): lax.ppermute(x, axis, [(i, i ^ 1 << apart) for i in range(lax.axis_size(a...  23.3 us
    ppermute x5, starting transfers between devices, swapped(): lax.ppermute(x, axis, [(i, i ^ 1 << apart) for i in range(lax.axis_size(a...  11.5 us
    psum x1, blocking collectives, on_device(): gains = lax.psum(jnp.stack(group_rows), ('inner', 'sub'))  10.7 us
    gather x3, local copies, waits for them, and re-layouts, on_device(): jnp.take(jnp.concatenate([first_sims, second_sims], 1), picked, axis=1)  7.26 us
    gather x1, local copies, waits for them, and re-layouts, on_device(): jnp.take(jnp.concatenate([first_rows, second_rows], 0), picked, axis=0)  3.94 us
    concatenate x2, local copies, waits for them, and re-layouts, on_device(): jnp.concatenate([first_sims, second_sims], 1)  3.84 us
    concatenate x2, other arithmetic, on_device(): jnp.concatenate([first_sims, second_sims], 1)  3 us
    dot_general x2, matrix products, on_device(): jnp.dot(points, partner.T, preferred_element_type=jnp.float32)  1.97 us
  transfers between devices with their start and end apart: 5, of which 4 were waited for; matrix products, arithmetic and copies ran while one was open for 26% of the time, Pallas kernels for 0%

commit v1 on v0

v1 whole, which is shorter than its diff:
```python
import functools

import jax
import jax.numpy as jnp
from jax import lax
from jax.experimental import pallas as pl
from jax.experimental.pallas import tpu as pltpu
from jax.sharding import PartitionSpec as P

MESH = pl.DeviceIdType.MESH
LANES = 128
CHUNK = 32
LOW = -1e30


def flipped(index, offset):
    out, bit = index, 1
    while bit <= offset:
        if offset & bit:
            out = out + bit * (1 - 2 * ((index // bit) % 2))
        bit *= 2
    return out


def as_row(tile):
    return jnp.concatenate([tile[k : k + 1] for k in range(tile.shape[0])], axis=1)


def as_tile(row):
    count = row.shape[1] // LANES
    return jnp.concatenate([row[:, k * LANES : (k + 1) * LANES] for k in range(count)], axis=0)


def marked(sel_tile, slots):
    sel = as_row(sel_tile)
    width = sel.shape[1]
    high, low = sel // LANES, sel % LANES
    tall = 2 * width // LANES
    high_hot = jnp.where(lax.broadcasted_iota(jnp.int32, (tall, width), 0) == high, 1.0, 0.0)
    if slots is not None:
        high_hot = high_hot * slots
    low_hot = jnp.where(lax.broadcasted_iota(jnp.int32, (LANES, width), 0) == low, 1.0, 0.0)
    return lax.dot_general(
        high_hot.astype(jnp.bfloat16),
        low_hot.astype(jnp.bfloat16),
        (((1,), (1,)), ((), ())),
        preferred_element_type=jnp.float32,
    )


def pick(table, index):
    high, low = index // LANES, index % LANES
    out = jnp.zeros(index.shape, table.dtype)
    for k in range(table.shape[0]):
        row = jnp.broadcast_to(table[k : k + 1], index.shape)
        value = jnp.take_along_axis(row, low, axis=1, mode="promise_in_bounds")
        out = jnp.where(high == k, value, out)
    return out


def kernel(
    levels, inner, sub,
    points, exemplars, selection, gains, cover,
    pts_in, sel_in, sims, bias, cov_out, cov_in, column, best, part_out, part_in, total_out, total_in,
    pts_send, pts_recv, sel_send, sel_recv, cov_send, cov_recv, part_send, part_recv, total_send, total_recv,
):
    span = 2**levels
    mates = inner * sub
    width = exemplars.shape[1]
    count = points.shape[0]
    tall = width // LANES
    my_leaf = lax.axis_index("leaf")
    bits = [(my_leaf // 2**height) % 2 for height in range(levels)]
    my_mate = lax.axis_index("inner") * sub + lax.axis_index("sub")

    leaf_ids = {d: {"leaf": flipped(my_leaf, d)} for d in range(1, span)}
    mate_ids = {}
    for k in range(1, mates):
        other = (my_mate + k) % mates
        mate_ids[k] = {"inner": other // sub, "sub": other % sub}

    barrier = pltpu.get_barrier_semaphore()
    for target in [*leaf_ids.values(), *mate_ids.values()]:
        pl.semaphore_signal(barrier, inc=1, device_id=target, device_id_type=MESH)
    pl.semaphore_wait(barrier, span - 1 + mates - 1)

    started = []

    def send(src, dst, send_sem, recv_sem, target):
        copy = pltpu.make_async_remote_copy(
            src_ref=src, dst_ref=dst, send_sem=send_sem, recv_sem=recv_sem,
            device_id=target, device_id_type=MESH,
        )
        copy.start()
        started.append(copy)
        return copy

    pts_copy, sel_copy, cov_copy, part_copy, total_copy = {}, {}, {}, {}, {}
    for d in range(1, span):
        pts_copy[d] = send(points, pts_in.at[d], pts_send.at[d], pts_recv.at[d], leaf_ids[d])
    for d in range(1, span):
        sel_copy[d] = send(selection, sel_in.at[d], sel_send.at[d], sel_recv.at[d], leaf_ids[d])

    def multiply(d):
        block = points if d == 0 else pts_in.at[d]
        sims[d] = lax.dot_general(
            block[...], exemplars[0], (((1,), (1,)), ((), ())), preferred_element_type=jnp.float32
        )

    def row_best(level, d):
        def body(i, carry):
            rows = pl.ds(pl.multiple_of(i * CHUNK, CHUNK), CHUNK)
            top = None
            for k in range(tall):
                lanes = pl.ds(k * LANES, LANES)
                value = sims[d, rows, lanes]
                if level > 0:
                    value = value + bias[level : level + 1, lanes]
                top = value if top is None else jnp.maximum(top, value)
            best[rows, :] = top
            return carry

        lax.fori_loop(0, count // CHUNK, body, 0)
        cov_out[level, d : d + 1] = jnp.max(best[...].T, axis=0, keepdims=True)

    def gain_sum(level, d, acc):
        row = None
        for s in range(span):
            if s >> level == d >> level:
                value = cov_out[level, d : d + 1] if s == 0 else cov_in[s, level, d ^ s : (d ^ s) + 1]
                row = value if row is None else jnp.maximum(row, value)
        column[...] = jnp.broadcast_to(row, (LANES, count)).T

        def body(i, total):
            rows = pl.ds(pl.multiple_of(i * CHUNK, CHUNK), CHUNK)
            base = column[rows, :]
            out = []
            for k in range(tall):
                value = jnp.maximum(sims[d, rows, k * LANES : (k + 1) * LANES] - base, 0.0)
                out.append(total[k] + value.reshape(CHUNK // 8, 8, LANES).sum(0))
            return tuple(out)

        return lax.fori_loop(0, count // CHUNK, body, acc)

    def finish(level, acc):
        part_out[level] = jnp.concatenate([jnp.sum(a, axis=0, keepdims=True) for a in acc], axis=0)

    def send_cov(level):
        for d in range(1, min(2 ** (level + 1), span)):
            cov_copy[level, d] = send(
                cov_out.at[level], cov_in.at[d, level], cov_send.at[level, d], cov_recv.at[level, d], leaf_ids[d]
            )

    none = tuple(jnp.zeros((8, LANES), jnp.float32) for _ in range(tall))

    multiply(0)
    row_best(0, 0)
    send_cov(0)
    for level in range(1, levels + 1):
        slots = None
        for height in reversed(range(level)):
            hits = marked(selection[height], slots)
            slots = as_row(jnp.where(bits[height] == 1, hits[tall:], hits[:tall]))
        bias[level : level + 1] = jnp.where(slots > 0.5, 0.0, LOW)

    for level in range(1, levels + 1):
        reach = 2**level
        last = level == levels
        if not last:
            for d in range(reach // 2, reach):
                pts_copy[d].wait_recv()
                multiply(d)
            for d in range(reach):
                row_best(level, d)
            send_cov(level)
        for d in range(1, reach):
            cov_copy[level - 1, d].wait_recv()
        acc = none
        for d in range(reach):
            if last and d >= reach // 2:
                pts_copy[d].wait_recv()
                multiply(d)
            acc = gain_sum(level - 1, d, acc)
        finish(level - 1, acc)

    for k in range(1, mates):
        part_copy[k] = send(part_out, part_in.at[k], part_send.at[k], part_recv.at[k], mate_ids[k])
    for d in range(span):
        row_best(levels, d)
    send_cov(levels)

    total = part_out[...]
    for k in range(1, mates):
        part_copy[k].wait_recv()
        total = total + part_in[k]
    total_out[...] = total
    for d in range(1, span):
        total_copy[d] = send(total_out, total_in.at[d], total_send.at[d], total_recv.at[d], leaf_ids[d])

    top = cov_out[levels, 0:1]
    for d in range(1, span):
        cov_copy[levels, d].wait_recv()
        top = jnp.maximum(top, cov_in[d, levels, d : d + 1])
    cover[...] = as_tile(top)

    for d in range(1, span):
        sel_copy[d].wait_recv()
        total_copy[d].wait_recv()
    for level in range(levels):
        blocks = [total_out[level] if d == 0 else total_in[d, level] for d in range(2 ** (level + 1))]
        for height in range(level + 1):
            step = 2**height
            for d in range(0, len(blocks), 2 * step):
                upper = bits[height] == 1
                mine, theirs = blocks[d], blocks[d + step]
                merged = jnp.concatenate(
                    [jnp.where(upper, theirs, mine), jnp.where(upper, mine, theirs)], axis=0
                )
                if height == level:
                    gains[level] = merged
                else:
                    blocks[d] = pick(merged, selection[height] if d == 0 else sel_in[d, height])
    for copy in started:
        copy.wait_send()


def on_device(points, exemplars, selection):
    levels = selection.shape[0]
    span = 2**levels
    inner, sub = lax.axis_size("inner"), lax.axis_size("sub")
    mates = inner * sub
    count, dim = points.shape
    width = exemplars.shape[1]
    tall = width // LANES
    cov_rows = max(8, span)
    f32 = jnp.float32
    dma = pltpu.SemaphoreType.DMA
    vmem = pl.BlockSpec(memory_space=pltpu.VMEM)
    gains, cover = pl.pallas_call(
        functools.partial(kernel, levels, inner, sub),
        out_shape=(
            jax.ShapeDtypeStruct((levels, 2 * tall, LANES), f32),
            jax.ShapeDtypeStruct((count // LANES, LANES), f32),
        ),
        in_specs=[vmem] * 3,
        out_specs=(vmem, vmem),
        scratch_shapes=[
            pltpu.VMEM((span, count, dim), points.dtype),
            pltpu.VMEM((span, levels, tall, LANES), jnp.int32),
            pltpu.VMEM((span, count, width), f32),
            pltpu.VMEM((max(8, levels + 1), width), f32),
            pltpu.VMEM((levels + 1, cov_rows, count), f32),
            pltpu.VMEM((span, levels + 1, cov_rows, count), f32),
            pltpu.VMEM((count, LANES), f32),
            pltpu.VMEM((count, LANES), f32),
            pltpu.VMEM((levels, tall, LANES), f32),
            pltpu.VMEM((mates, levels, tall, LANES), f32),
            pltpu.VMEM((levels, tall, LANES), f32),
            pltpu.VMEM((span, levels, tall, LANES), f32),
            dma((span,)), dma((span,)),
            dma((span,)), dma((span,)),
            dma((levels + 1, span)), dma((levels + 1, span)),
            dma((mates,)), dma((mates,)),
            dma((span,)), dma((span,)),
        ],
        compiler_params=pltpu.CompilerParams(
            collective_id=0, has_side_effects=True, vmem_limit_bytes=48 * 1024 * 1024
        ),
    )(points, exemplars, selection.reshape(levels, tall, LANES))
    return gains.reshape(levels, 1, 2 * width), cover.reshape(count)


def solution(mesh):
    placed = (
        P(("parts", "leaf", "inner", "sub"), None),
        P(("parts", "leaf"), None, None),
        P(None, ("parts", "leaf"), None),
    )
    return jax.shard_map(
        on_device,
        mesh=mesh,
        in_specs=placed,
        out_specs=(P(None, ("parts", "leaf"), None), P(("parts", "leaf", "inner", "sub"))),
        check_vma=False,
    )
```

time: 71.8 us -> 32.8 us (0.46)
  Pallas kernels: 0 us -> 28.1 us
  waiting for transfers between devices: 23.3 us -> 0 us
  local copies, waits for them, and re-layouts: 15.8 us -> 3.81 us
  starting transfers between devices: 11.5 us -> 0 us
  blocking collectives: 10.7 us -> 0 us
  other arithmetic: 5.85 us -> 0 us
  matrix products: 3.42 us -> 0 us
    pallas_call x0 -> x1, Pallas kernels: none -> 28.1 us  [on_device(): pl.pallas_call(functools.partial(kernel, levels, inner, sub), out_shape=(...]
    ppermute x5 -> x0, waiting for transfers between devices: 23.3 us -> none  [swapped(): lax.ppermute(x, axis, [(i, i ^ 1 << apart) for i in range(lax.axis_size(a...]
    ppermute x5 -> x0, starting transfers between devices: 11.5 us -> none  [swapped(): lax.ppermute(x, axis, [(i, i ^ 1 << apart) for i in range(lax.axis_size(a...]
    gather x4 -> x0, local copies, waits for them, and re-layouts: 11.2 us -> none  [the longest x3 7.26 us: on_device(): jnp.take(jnp.concatenate([first_sims, second_sims], 1), picked, axis=1)]
    psum x1 -> x0, blocking collectives: 10.7 us -> none  [on_device(): gains = lax.psum(jnp.stack(group_rows), ('inner', 'sub'))]
    concatenate x2 -> x0, local copies, waits for them, and re-layouts: 3.84 us -> none  [on_device(): jnp.concatenate([first_sims, second_sims], 1)]
    unnamed x4 -> x8, local copies, waits for them, and re-layouts: 0.02 us -> 3.81 us
    dot_general x3 -> x0, matrix products: 3.42 us -> none  [the longest x2 1.97 us: on_device(): jnp.dot(points, partner.T, preferred_element_type=jnp.float32)]
  transfers between devices with their start and end apart: 5 -> 0, of which waited for: 4 -> 0; matrix products, arithmetic and copies ran while one was open for 26% -> 0% of each run, Pallas kernels for 0% -> 0%
where the time goes in v1:
time: 32.8 us; the launch traced here: 32.5 us
  Pallas kernels  28.1 us (86%)
  local copies, waits for them, and re-layouts  3.81 us (12%)
  between operations  0.65 us (2%)
    pallas_call x1, Pallas kernels, on_device(): pl.pallas_call(functools.partial(kernel, levels, inner, sub), out_shape=(...  28.1 us
    unnamed x8, local copies, waits for them, and re-layouts  3.81 us

profile of v1, /device:TPU:0, one launch (start us, length us, event | category | flops | bytes accessed | tf_op | source)
XLA Modules:
  0.0 32.5 jit_solution(1665885454925229556)
XLA Ops:
  0.6 0.0 copy-start
  0.6 1.0 %copy-done = bf16[1,1024,256]{2,1,0:T(8,128)(2,1)S(1)} copy-done((bf16[1,1024,256]{2,1,0:T(8,128)(2,1)S(1)}, bf16[1,1024,256]{2,1,0:T(8,128)(2,1)}, u32[]{:S(2)}) %copy-start) | copy-done | bytes 524312
  1.7 0.0 copy-start.1
  1.7 0.9 %copy-done.1 = bf16[256,256]{1,0:T(8,128)(2,1)S(1)} copy-done((bf16[256,256]{1,0:T(8,128)(2,1)S(1)}, bf16[256,256]{1,0:T(8,128)(2,1)}, u32[]{:S(2)}) %copy-start.1) | copy-done | bytes 131096
  2.6 0.0 copy-start.2
  2.6 0.7 %copy-done.2 = s32[2,1,1024]{2,1,0:T(1,128)S(1)} copy-done((s32[2,1,1024]{2,1,0:T(1,128)S(1)}, s32[2,1,1024]{2,1,0:T(1,128)}, u32[]{:S(2)}) %copy-start.2) | copy-done | bytes 8216
  3.3 28.1 %shard_map.50 = (f32[2,16,128]{2,1,0:T(8,128)S(1)}, f32[2,128]{1,0:T(2,128)S(1)}) custom-call(bf16[256,256]{1,0:T(8,128)(2,1)S(1)} %copy-done.1, bf16[1,1024,256]{2,1,0:T(8,128)(2,1)S(1)} %copy-done, s32[2,8,128]{2,1,0:T(8,128)S(1)} %bitcast.4), custom_call_target="tpu_custom_call" | custom-call | tf_op jit(solution)/shard_map/pallas_call | solution.py:239
  31.4 0.6 %copy.8 = f32[2,1,2048]{2,1,0:T(1,128)} copy(f32[2,1,2048]{2,1,0:T(1,128)S(1)} %bitcast.3) | data formatting | bytes 32768
  32.0 0.6 %copy.9 = f32[256]{0:T(256)} copy(f32[256]{0:T(256)S(1)} %bitcast.5) | data formatting | bytes 2048
Async XLA Ops:
  0.6 1.0 %copy-start = (bf16[1,1024,256]{2,1,0:T(8,128)(2,1)S(1)}, bf16[1,1024,256]{2,1,0:T(8,128)(2,1)}, u32[]{:S(2)}) copy-start(bf16[1,1024,256]{2,1,0:T(8,128)(2,1)} %exemplars.1) | copy-start | bytes 1572868
  1.7 0.9 %copy-start.1 = (bf16[256,256]{1,0:T(8,128)(2,1)S(1)}, bf16[256,256]{1,0:T(8,128)(2,1)}, u32[]{:S(2)}) copy-start(bf16[256,256]{1,0:T(8,128)(2,1)} %points.1) | copy-start | bytes 393220
  2.6 0.7 %copy-start.2 = (s32[2,1,1024]{2,1,0:T(1,128)S(1)}, s32[2,1,1024]{2,1,0:T(1,128)}, u32[]{:S(2)}) copy-start(s32[2,1,1024]{2,1,0:T(1,128)} %param.5) | copy-start | bytes 24580

commit v2 on v1

--- a/solution.py
+++ b/solution.py
@@ -10,6 +10,7 @@
 MESH = pl.DeviceIdType.MESH
 LANES = 128
 CHUNK = 32
+PARTS = 4
 LOW = -1e30
 
 
@@ -61,8 +62,9 @@
 def kernel(
     levels, inner, sub,
     points, exemplars, selection, gains, cover,
-    pts_in, sel_in, sims, bias, cov_out, cov_in, column, best, part_out, part_in, total_out, total_in,
-    pts_send, pts_recv, sel_send, sel_recv, cov_send, cov_recv, part_send, part_recv, total_send, total_recv,
+    pts_in, ex_in, sel_own, sel_in, sims, bias, cov_out, cov_in, last_out, last_in, column, best,
+    part_out, part_in, total_out, total_in,
+    fetch_sem, pts_send, pts_recv, sel_send, sel_recv, cov_send, cov_recv, last_send, last_recv, part_send, part_recv, total_send, total_recv,
 ):
     span = 2**levels
     mates = inner * sub
@@ -79,10 +81,21 @@
         other = (my_mate + k) % mates
         mate_ids[k] = {"inner": other // sub, "sub": other % sub}
 
+    here = my_leaf % span
+
+    def block_of(d):
+        return flipped(here, d)
+
     barrier = pltpu.get_barrier_semaphore()
     for target in [*leaf_ids.values(), *mate_ids.values()]:
         pl.semaphore_signal(barrier, inc=1, device_id=target, device_id_type=MESH)
-    pl.semaphore_wait(barrier, span - 1 + mates - 1)
+    fetches = [
+        pltpu.make_async_copy(points, pts_in.at[here], fetch_sem.at[0]),
+        pltpu.make_async_copy(exemplars.at[0], ex_in, fetch_sem.at[1]),
+        pltpu.make_async_copy(selection, sel_own, fetch_sem.at[2]),
+    ]
+    for fetch in fetches:
+        fetch.start()
 
     started = []
 
@@ -95,16 +108,49 @@
         started.append(copy)
         return copy
 
-    pts_copy, sel_copy, cov_copy, part_copy, total_copy = {}, {}, {}, {}, {}
-    for d in range(1, span):
-        pts_copy[d] = send(points, pts_in.at[d], pts_send.at[d], pts_recv.at[d], leaf_ids[d])
-    for d in range(1, span):
-        sel_copy[d] = send(selection, sel_in.at[d], sel_send.at[d], sel_recv.at[d], leaf_ids[d])
+    sel_copy, cov_copy, last_copy, part_copy, total_copy = {}, {}, {}, {}, {}
+
+    def passing(slot, part, side):
+        rows = pl.ds(part * (count // PARTS), count // PARTS)
+        return pltpu.make_async_remote_copy(
+            src_ref=pts_in.at[slot, rows], dst_ref=pts_in.at[slot, rows],
+            send_sem=pts_send.at[side, slot, part], recv_sem=pts_recv.at[slot, part],
+            device_id={"leaf": my_leaf + 2 * side - 1}, device_id_type=MESH,
+        )
+
+    has_side = [here > 0, here < span - 1]
+
+    def relay(distance, act):
+        for part in range(PARTS):
+            for side in (1, 0):
+                slot = here - distance if side == 1 else here + distance
+                inside = slot >= 0 if side == 1 else slot < span
+
+                @pl.when(inside)
+                def _():
+                    copy = passing(slot, part, side)
+                    act(copy, side)
+
+    def arrive_and_pass(copy, side):
+        copy.wait_recv()
+
+        @pl.when(has_side[side])
+        def _():
+            copy.start()
+
+    def start_own(copy, side):
+        @pl.when(has_side[side])
+        def _():
+            copy.start()
+
+    def finish_pass(copy, side):
+        @pl.when(has_side[side])
+        def _():
+            copy.wait_send()
 
     def multiply(d):
-        block = points if d == 0 else pts_in.at[d]
         sims[d] = lax.dot_general(
-            block[...], exemplars[0], (((1,), (1,)), ((), ())), preferred_element_type=jnp.float32
+            pts_in[block_of(d)], ex_in[...], (((1,), (1,)), ((), ())), preferred_element_type=jnp.float32
         )
 
     def row_best(level, d):
@@ -121,7 +167,15 @@
             return carry
 
         lax.fori_loop(0, count // CHUNK, body, 0)
-        cov_out[level, d : d + 1] = jnp.max(best[...].T, axis=0, keepdims=True)
+        row = jnp.max(best[...].T, axis=0, keepdims=True)
+        if level == levels:
+            last_out[d] = as_tile(row)
+            if d > 0:
+                last_copy[d] = send(
+                    last_out.at[d], last_in.at[d], last_send.at[d], last_recv.at[d], leaf_ids[d]
+                )
+        else:
+            cov_out[level, d : d + 1] = row
 
     def gain_sum(level, d, acc):
         row = None
@@ -153,41 +207,49 @@
 
     none = tuple(jnp.zeros((8, LANES), jnp.float32) for _ in range(tall))
 
+    fetches[0].wait()
+    fetches[1].wait()
     multiply(0)
     row_best(0, 0)
+    pl.semaphore_wait(barrier, span - 1 + mates - 1)
+    relay(0, start_own)
     send_cov(0)
+    fetches[2].wait()
     for level in range(1, levels + 1):
         slots = None
         for height in reversed(range(level)):
-            hits = marked(selection[height], slots)
+            hits = marked(sel_own[height], slots)
             slots = as_row(jnp.where(bits[height] == 1, hits[tall:], hits[:tall]))
         bias[level : level + 1] = jnp.where(slots > 0.5, 0.0, LOW)
 
-    for level in range(1, levels + 1):
-        reach = 2**level
-        last = level == levels
-        if not last:
-            for d in range(reach // 2, reach):
-                pts_copy[d].wait_recv()
-                multiply(d)
-            for d in range(reach):
-                row_best(level, d)
-            send_cov(level)
-        for d in range(1, reach):
-            cov_copy[level - 1, d].wait_recv()
-        acc = none
-        for d in range(reach):
-            if last and d >= reach // 2:
-                pts_copy[d].wait_recv()
-                multiply(d)
-            acc = gain_sum(level - 1, d, acc)
-        finish(level - 1, acc)
+    level, acc = 1, none
+    for d in range(1, span):
+        relay(d, arrive_and_pass)
+        if d == 2 ** (level - 1) :
+            for e in range(1, d + d):
+                cov_copy[level - 1, e].wait_recv()
+            acc = none
+            for e in range(d):
+                acc = gain_sum(level - 1, e, acc)
+        multiply(d)
+        acc = gain_sum(level - 1, d, acc)
+        if d == 2**level - 1:
+            finish(level - 1, acc)
+            if level < levels:
+                for e in range(d + 1):
+                    row_best(level, e)
+                send_cov(level)
+                if level == levels - 1:
+                    for e in range(d + 1):
+                        row_best(levels, e)
+            level += 1
 
     for k in range(1, mates):
         part_copy[k] = send(part_out, part_in.at[k], part_send.at[k], part_recv.at[k], mate_ids[k])
-    for d in range(span):
+    for d in range(2, span, 2):
+        sel_copy[d] = send(sel_own, sel_in.at[d], sel_send.at[d], sel_recv.at[d], leaf_ids[d])
+    for d in range(span // 2 if levels > 1 else 0, span):
         row_best(levels, d)
-    send_cov(levels)
 
     total = part_out[...]
     for k in range(1, mates):
@@ -197,15 +259,16 @@
     for d in range(1, span):
         total_copy[d] = send(total_out, total_in.at[d], total_send.at[d], total_recv.at[d], leaf_ids[d])
 
-    top = cov_out[levels, 0:1]
+    top = last_out[0]
     for d in range(1, span):
-        cov_copy[levels, d].wait_recv()
-        top = jnp.maximum(top, cov_in[d, levels, d : d + 1])
-    cover[...] = as_tile(top)
+        last_copy[d].wait_recv()
+        top = jnp.maximum(top, last_in[d])
+    cover[...] = top
 
     for d in range(1, span):
-        sel_copy[d].wait_recv()
         total_copy[d].wait_recv()
+    for copy in sel_copy.values():
+        copy.wait_recv()
     for level in range(levels):
         blocks = [total_out[level] if d == 0 else total_in[d, level] for d in range(2 ** (level + 1))]
         for height in range(level + 1):
@@ -219,9 +282,16 @@
                 if height == level:
                     gains[level] = merged
                 else:
-                    blocks[d] = pick(merged, selection[height] if d == 0 else sel_in[d, height])
+                    blocks[d] = pick(merged, sel_own[height] if d == 0 else sel_in[d, height])
     for copy in started:
         copy.wait_send()
+    for distance in range(span - 1):
+        relay(distance, finish_pass)
+
+
+def hand_out(gains_in, cover_in, gains, cover):
+    gains[...] = gains_in[...]
+    cover[...] = cover_in[...]
 
 
 def on_device(points, exemplars, selection):
@@ -242,31 +312,43 @@
             jax.ShapeDtypeStruct((levels, 2 * tall, LANES), f32),
             jax.ShapeDtypeStruct((count // LANES, LANES), f32),
         ),
-        in_specs=[vmem] * 3,
+        in_specs=[pl.BlockSpec(memory_space=pltpu.HBM)] * 3,
         out_specs=(vmem, vmem),
         scratch_shapes=[
             pltpu.VMEM((span, count, dim), points.dtype),
+            pltpu.VMEM((width, dim), exemplars.dtype),
+            pltpu.VMEM((levels, tall, LANES), jnp.int32),
             pltpu.VMEM((span, levels, tall, LANES), jnp.int32),
             pltpu.VMEM((span, count, width), f32),
             pltpu.VMEM((max(8, levels + 1), width), f32),
-            pltpu.VMEM((levels + 1, cov_rows, count), f32),
-            pltpu.VMEM((span, levels + 1, cov_rows, count), f32),
+            pltpu.VMEM((levels, cov_rows, count), f32),
+            pltpu.VMEM((span, levels, cov_rows, count), f32),
+            pltpu.VMEM((span, count // LANES, LANES), f32),
+            pltpu.VMEM((span, count // LANES, LANES), f32),
             pltpu.VMEM((count, LANES), f32),
             pltpu.VMEM((count, LANES), f32),
             pltpu.VMEM((levels, tall, LANES), f32),
             pltpu.VMEM((mates, levels, tall, LANES), f32),
             pltpu.VMEM((levels, tall, LANES), f32),
             pltpu.VMEM((span, levels, tall, LANES), f32),
+            dma((3,)),
+            dma((2, span, PARTS)), dma((span, PARTS)),
             dma((span,)), dma((span,)),
+            dma((levels, span)), dma((levels, span)),
             dma((span,)), dma((span,)),
-            dma((levels + 1, span)), dma((levels + 1, span)),
             dma((mates,)), dma((mates,)),
             dma((span,)), dma((span,)),
         ],
         compiler_params=pltpu.CompilerParams(
-            collective_id=0, has_side_effects=True, vmem_limit_bytes=48 * 1024 * 1024
+            collective_id=0, has_side_effects=True, vmem_limit_bytes=64 * 1024 * 1024 - 65536
         ),
     )(points, exemplars, selection.reshape(levels, tall, LANES))
+    gains, cover = pl.pallas_call(
+        hand_out,
+        out_shape=tuple(jax.ShapeDtypeStruct(x.shape, x.dtype) for x in (gains, cover)),
+        in_specs=[vmem] * 2,
+        out_specs=(vmem, vmem),
+    )(gains, cover)
     return gains.reshape(levels, 1, 2 * width), cover.reshape(count)
 
 

time: 32.8 us -> 26.9 us (0.82)
  local copies, waits for them, and re-layouts: 3.81 us -> 0 us
  Pallas kernels: 28.1 us -> 26 us
    unnamed x8 -> x0, local copies, waits for them, and re-layouts: 3.81 us -> none
    pallas_call x1, Pallas kernels: 28.1 us -> 24.7 us  [on_device(): pl.pallas_call(functools.partial(kernel, levels, inner, sub), out_shape=(...]
    pallas_call x0 -> x1, Pallas kernels: none -> 1.33 us  [on_device(): pl.pallas_call(hand_out, out_shape=tuple((jax.ShapeDtypeStruct(x.shape, x...]
where the time goes in v2:
time: 26.9 us; the launch traced here: 26.6 us
  Pallas kernels  26 us (97%)
  between operations  0.64 us (2%)
    pallas_call x1, Pallas kernels, on_device(): pl.pallas_call(functools.partial(kernel, levels, inner, sub), out_shape=(...  24.7 us
    pallas_call x1, Pallas kernels, on_device(): pl.pallas_call(hand_out, out_shape=tuple((jax.ShapeDtypeStruct(x.shape, x...  1.33 us

profile of v2, /device:TPU:0, one launch (start us, length us, event | category | flops | bytes accessed | tf_op | source)
XLA Modules:
  0.0 26.6 jit_solution(6375109941613045570)
XLA Ops:
  0.6 24.7 %shard_map.50 = (f32[2,16,128]{2,1,0:T(8,128)}, f32[2,128]{1,0:T(2,128)}) custom-call(bf16[256,256]{1,0:T(8,128)(2,1)} %points.1, bf16[1,1024,256]{2,1,0:T(8,128)(2,1)} %exemplars.1, s32[2,8,128]{2,1,0:T(8,128)} %bitcast.3), custom_call_target="tpu_custom_call" | custom-call | tf_op jit(solution)/shard_map/pallas_call | solution.py:309
  25.3 1.3 %shard_map.51 = (f32[2,16,128]{2,1,0:T(8,128)}, f32[2,128]{1,0:T(2,128)}) custom-call(f32[2,16,128]{2,1,0:T(8,128)} %get-tuple-element.6.gains_in, f32[2,128]{1,0:T(2,128)} %get-tuple-element.7.cover_in), custom_call_target="tpu_custom_call" | custom-call | tf_op jit(solution)/shard_map/pallas_call | solution.py:346

commit v3 on v2

--- a/solution.py
+++ b/solution.py
@@ -63,8 +63,8 @@
     levels, inner, sub,
     points, exemplars, selection, gains, cover,
     pts_in, ex_in, sel_own, sel_in, sims, bias, cov_out, cov_in, last_out, last_in, column, best,
-    part_out, part_in, total_out, total_in,
-    fetch_sem, pts_send, pts_recv, sel_send, sel_recv, cov_send, cov_recv, last_send, last_recv, part_send, part_recv, total_send, total_recv,
+    part_out, part_in, totals,
+    fetch_sem, pts_send, pts_recv, sel_send, sel_recv, cov_send, cov_recv, last_send, last_recv, part_send, part_recv,
 ):
     span = 2**levels
     mates = inner * sub
@@ -87,7 +87,12 @@
         return flipped(here, d)
 
     barrier = pltpu.get_barrier_semaphore()
-    for target in [*leaf_ids.values(), *mate_ids.values()]:
+    all_ids = {}
+    for d in range(span):
+        for k in range(mates):
+            if d + k > 0:
+                all_ids[d, k] = {**leaf_ids.get(d, {}), **mate_ids.get(k, {})}
+    for target in all_ids.values():
         pl.semaphore_signal(barrier, inc=1, device_id=target, device_id_type=MESH)
     fetches = [
         pltpu.make_async_copy(points, pts_in.at[here], fetch_sem.at[0]),
@@ -108,7 +113,7 @@
         started.append(copy)
         return copy
 
-    sel_copy, cov_copy, last_copy, part_copy, total_copy = {}, {}, {}, {}, {}
+    sel_copy, cov_copy, last_copy, part_copy = {}, {}, {}, {}
 
     def passing(slot, part, side):
         rows = pl.ds(part * (count // PARTS), count // PARTS)
@@ -211,7 +216,7 @@
     fetches[1].wait()
     multiply(0)
     row_best(0, 0)
-    pl.semaphore_wait(barrier, span - 1 + mates - 1)
+    pl.semaphore_wait(barrier, span * mates - 1)
     relay(0, start_own)
     send_cov(0)
     fetches[2].wait()
@@ -244,20 +249,16 @@
                         row_best(levels, e)
             level += 1
 
-    for k in range(1, mates):
-        part_copy[k] = send(part_out, part_in.at[k], part_send.at[k], part_recv.at[k], mate_ids[k])
+    for d in reversed(range(span)):
+        for k in range(mates):
+            if d + k > 0:
+                part_copy[d, k] = send(
+                    part_out, part_in.at[d, k], part_send.at[d, k], part_recv.at[d, k], all_ids[d, k]
+                )
     for d in range(2, span, 2):
         sel_copy[d] = send(sel_own, sel_in.at[d], sel_send.at[d], sel_recv.at[d], leaf_ids[d])
     for d in range(span // 2 if levels > 1 else 0, span):
         row_best(levels, d)
-
-    total = part_out[...]
-    for k in range(1, mates):
-        part_copy[k].wait_recv()
-        total = total + part_in[k]
-    total_out[...] = total
-    for d in range(1, span):
-        total_copy[d] = send(total_out, total_in.at[d], total_send.at[d], total_recv.at[d], leaf_ids[d])
 
     top = last_out[0]
     for d in range(1, span):
@@ -265,12 +266,17 @@
         top = jnp.maximum(top, last_in[d])
     cover[...] = top
 
-    for d in range(1, span):
-        total_copy[d].wait_recv()
+    for d in range(span):
+        total = part_out[...] if d == 0 else None
+        for k in range(mates):
+            if d + k > 0:
+                part_copy[d, k].wait_recv()
+                total = part_in[d, k] if total is None else total + part_in[d, k]
+        totals[d] = total
     for copy in sel_copy.values():
         copy.wait_recv()
     for level in range(levels):
-        blocks = [total_out[level] if d == 0 else total_in[d, level] for d in range(2 ** (level + 1))]
+        blocks = [totals[d, level] for d in range(2 ** (level + 1))]
         for height in range(level + 1):
             step = 2**height
             for d in range(0, len(blocks), 2 * step):
@@ -328,16 +334,14 @@
             pltpu.VMEM((count, LANES), f32),
             pltpu.VMEM((count, LANES), f32),
             pltpu.VMEM((levels, tall, LANES), f32),
-            pltpu.VMEM((mates, levels, tall, LANES), f32),
-            pltpu.VMEM((levels, tall, LANES), f32),
+            pltpu.VMEM((span, mates, levels, tall, LANES), f32),
             pltpu.VMEM((span, levels, tall, LANES), f32),
             dma((3,)),
             dma((2, span, PARTS)), dma((span, PARTS)),
             dma((span,)), dma((span,)),
             dma((levels, span)), dma((levels, span)),
             dma((span,)), dma((span,)),
-            dma((mates,)), dma((mates,)),
-            dma((span,)), dma((span,)),
+            dma((span, mates)), dma((span, mates)),
         ],
         compiler_params=pltpu.CompilerParams(
             collective_id=0, has_side_effects=True, vmem_limit_bytes=64 * 1024 * 1024 - 65536

time: 26.9 us -> 26.2 us (0.974)
  Pallas kernels: 26 us -> 25.3 us
    pallas_call x1, Pallas kernels: 24.7 us -> 24 us  [on_device(): pl.pallas_call(functools.partial(kernel, levels, inner, sub), out_shape=(...]
where the time goes in v3:
time: 26.2 us; the launch traced here: 26 us
  Pallas kernels  25.3 us (97%)
  between operations  0.64 us (2%)
    pallas_call x1, Pallas kernels, on_device(): pl.pallas_call(functools.partial(kernel, levels, inner, sub), out_shape=(...  24 us
    pallas_call x1, Pallas kernels, on_device(): pl.pallas_call(hand_out, out_shape=tuple((jax.ShapeDtypeStruct(x.shape, x...  1.33 us

profile of v3, /device:TPU:0, one launch (start us, length us, event | category | flops | bytes accessed | tf_op | source)
XLA Modules:
  0.0 26.0 jit_solution(9335888400434523707)
XLA Ops:
  0.6 24.0 %shard_map.50 = (f32[2,16,128]{2,1,0:T(8,128)}, f32[2,128]{1,0:T(2,128)}) custom-call(bf16[256,256]{1,0:T(8,128)(2,1)} %points.1, bf16[1,1024,256]{2,1,0:T(8,128)(2,1)} %exemplars.1, s32[2,8,128]{2,1,0:T(8,128)} %bitcast.3), custom_call_target="tpu_custom_call" | custom-call | tf_op jit(solution)/shard_map/pallas_call | solution.py:315
  24.6 1.3 %shard_map.51 = (f32[2,16,128]{2,1,0:T(8,128)}, f32[2,128]{1,0:T(2,128)}) custom-call(f32[2,16,128]{2,1,0:T(8,128)} %get-tuple-element.6.gains_in, f32[2,128]{1,0:T(2,128)} %get-tuple-element.7.cover_in), custom_call_target="tpu_custom_call" | custom-call | tf_op jit(solution)/shard_map/pallas_call | solution.py:350
